TPU v7x, 128 devices: a whole 4x4x4 slice. The times are simulated.
128 devices in a mesh: dp: 16 (over y, z), expert: 8 (over x, core).
Axes of the slice: x: 4, y: 4, z: 4, core: 2. Of those that a mesh axis runs over, the one named last changes fastest.
Arguments:
- grad_out: bfloat16 [16384, 6144], P(('dp', 'expert')), may hold values from -6 to 6
- routes: int32 [16384, 2], P(('dp', 'expert')), may hold values from 0 to 31, all different within a row; in each aligned block of 128 rows (0 to 127, 128 to 255, ...) at most 9 rows name the same one
- loss_weight: int32 [16384], P(('dp', 'expert')), may hold values from 1 to 4
- saved_input: bfloat16 [32, 1152, 6144], P('dp', None, 'expert'), may hold values from -6 to 6
- saved_gate: bfloat16 [32, 1152, 1024], P('dp', None, 'expert'), may hold values from -8 to 8
- saved_up: bfloat16 [32, 1152, 1024], P('dp', None, 'expert'), may hold values from -6 to 6
- w_gate: bfloat16 [32, 6144, 1024], P('dp', 'expert'), may hold values from -0.1875 to 0.1875
- w_up: bfloat16 [32, 6144, 1024], P('dp', 'expert'), may hold values from -0.1875 to 0.1875
- w_down: bfloat16 [32, 1024, 6144], P('dp', None, 'expert'), may hold values from -0.078125 to 0.078125
Outputs:
- grad_input: bfloat16 [16384, 6144], P(('dp', 'expert'))
- grad_gate: bfloat16 [32, 6144, 1024], P('dp', 'expert')
- grad_up: bfloat16 [32, 6144, 1024], P('dp', 'expert')
- grad_down: bfloat16 [32, 1024, 6144], P('dp', None, 'expert')
Inputs may be any that keep to these rules, and one draw needn't show every extreme that they name: `routes`: each row names two different experts; among the rows of one device no expert is named more than 9 times, and some device names some expert exactly 9 times.
All inputs are finite; a program needn't handle non-finite values.
Results may differ from a plain program's by a relative error of at most 0.0061.
Values may be sent and summed in bfloat16 or wider, within the bound.
No kernel may reach another device: no remote copies, remote signals or barrier semaphores. Data moves between devices by JAX's collectives and lax.ppermute only.
A program may use at most 192 MiB of HBM per device.

v0:
```python
import jax
import jax.numpy as jnp
from jax import lax
from jax.sharding import PartitionSpec as P


def body(grad_out, routes, loss_weight, saved_input, saved_gate, saved_up, w_gate, w_up, w_down):
    groups = lax.axis_size("dp")
    splits = lax.axis_size("expert")
    local_experts = w_gate.shape[0]
    experts_all = local_experts * groups
    tokens_here = grad_out.shape[0]
    width = grad_out.shape[1]
    slice_width = width // splits
    slots_all = saved_input.shape[1]
    capacity = slots_all // (groups * splits)
    scaled = (
        grad_out.astype(jnp.float32) * loss_weight.astype(jnp.float32)[:, None] * 0.25
    ).astype(jnp.bfloat16)
    chosen = routes.reshape(-1)
    onehot = (chosen[:, None] == jnp.arange(experts_all, dtype=jnp.int32)[None, :]).astype(
        jnp.int32
    )
    before = jnp.cumsum(onehot, axis=0) - onehot
    rank = jnp.sum(before * onehot, axis=1)
    dest_row = (chosen % local_experts * groups + chosen // local_experts) * capacity + rank
    marks = (
        dest_row[:, None] == jnp.arange(experts_all * capacity, dtype=jnp.int32)[None, :]
    ).astype(jnp.float32)
    placed = jnp.sum(marks.reshape(tokens_here, 2, experts_all * capacity), axis=1).astype(
        jnp.bfloat16
    )
    outgoing = jnp.einsum("tr,td->rd", placed, scaled, preferred_element_type=jnp.float32).astype(
        jnp.bfloat16
    )
    ordered = outgoing.reshape(local_experts, groups, capacity, splits, slice_width)
    ordered = ordered.transpose(0, 1, 3, 2, 4).reshape(
        local_experts, groups * splits, capacity, slice_width
    )
    arrived = lax.all_to_all(ordered, ("dp", "expert"), split_axis=1, concat_axis=1, tiled=True)
    dispatched = arrived.reshape(local_experts, slots_all, slice_width)
    partial_value = jnp.einsum(
        "esd,ehd->esh", dispatched, w_down, preferred_element_type=jnp.float32
    )
    dhidden = lax.psum(partial_value, "expert")
    gates_all, ups_all = (
        lax.all_gather(saved_gate, "expert", axis=2, tiled=True),
        lax.all_gather(saved_up, "expert", axis=2, tiled=True),
    )
    gvals = gates_all.astype(jnp.float32)
    uvals = ups_all.astype(jnp.float32)
    sig = jax.nn.sigmoid(gvals)
    act = gvals * sig
    hidden = (act * uvals).astype(jnp.bfloat16)
    dgate = (dhidden * uvals * sig * (1.0 + gvals * (1.0 - sig))).astype(jnp.bfloat16)
    dup = (dhidden * act).astype(jnp.bfloat16)
    hidden, dgate, dup = (hidden, dgate, dup)
    grad_down = jnp.einsum(
        "esh,esd->ehd", hidden, dispatched, preferred_element_type=jnp.float32
    ).astype(jnp.bfloat16)
    grad_gate = jnp.einsum(
        "esd,esh->edh", saved_input, dgate, preferred_element_type=jnp.float32
    ).astype(jnp.bfloat16)
    grad_up = jnp.einsum(
        "esd,esh->edh", saved_input, dup, preferred_element_type=jnp.float32
    ).astype(jnp.bfloat16)
    slot_grad = jnp.einsum("esh,edh->esd", dgate, w_gate, preferred_element_type=jnp.float32)
    slot_grad = slot_grad + jnp.einsum(
        "esh,edh->esd", dup, w_up, preferred_element_type=jnp.float32
    )
    slot_grad = slot_grad.astype(jnp.bfloat16)
    leaving = slot_grad.reshape(local_experts, groups * splits, capacity, slice_width)
    returned = lax.all_to_all(leaving, ("dp", "expert"), split_axis=1, concat_axis=1, tiled=True)
    returned = returned.reshape(local_experts, groups, splits, capacity, slice_width).transpose(
        0, 1, 3, 2, 4
    )
    returned = returned.reshape(experts_all * capacity, width)
    grad_input = jnp.einsum(
        "tr,rd->td", placed, returned, preferred_element_type=jnp.float32
    ).astype(jnp.bfloat16)
    return (grad_input, grad_gate, grad_up, grad_down)


def solution(mesh):
    return jax.shard_map(
        body,
        mesh=mesh,
        in_specs=(
            P(("dp", "expert"), None),
            P(("dp", "expert"), None),
            P(("dp", "expert")),
            P("dp", None, "expert"),
            P("dp", None, "expert"),
            P("dp", None, "expert"),
            P("dp", "expert", None),
            P("dp", "expert", None),
            P("dp", None, "expert"),
        ),
        out_specs=(
            P(("dp", "expert"), None),
            P("dp", "expert", None),
            P("dp", "expert", None),
            P("dp", None, "expert"),
        ),
        check_vma=False,
    )
```

profile of v0, /device:TPU:1, one launch (start us, length us, event | category | flops | bytes accessed | tf_op | source)
XLA Modules:
  0.0 385.4 jit_solution(1867682180642988697)
XLA Ops:
  7.2 1.6 copy.105
  8.8 1.0 eq.45
  9.8 1.0 eq.41
  12.0 1.9 reduce-window.6
  13.9 0.9 slice_reduce_fusion
  14.9 0.9 fusion.24
  15.8 0.8 reduce_sum.21
  16.5 0.9 copy.108
  17.4 0.7 multiply_add_fusion
  18.2 2.6 convolution_convert_fusion
  20.8 1.0 copy.124
  22.3 3.6 copy.110
  25.9 57.3 %all_to_all.10 = bf16[2,128,9,768]{3,0,2,1:T(2,128)(2,1)S(1)} all-to-all(bf16[2,128,9,768]{3,0,2,1:T(2,128)(2,1)S(1)} %copy.110), channel_id=1, replica_groups=mesh['dp'=16,'expert'=8] {'dp','expert'}, dimensions={1} | all-to-all | bytes 7077888 | tf_op jit(solution)/shard_map/all_to_all | solution.py:40
  83.3 1.9 copy-done.3
  85.1 6.2 %fusion.11 = f32[2,1152,1024]{2,1,0:T(8,128)} fusion(bf16[2,1024,768]{2,1,0:T(8,128)(2,1)S(1)} %copy-done.6, bf16[2,1152,768]{2,0,1:T(2,128)(2,1)S(1)} %bitcast.56), kind=kOutput, calls=%fused_computation.23 | convolution fusion | flops 3623878656 | bytes 16121856 | tf_op jit(solution)/shard_map/esd,ehd->esh/dot_general | solution.py:42
  92.8 108.4 %all-reduce.2.cloned.1.call-done = f32[2,1152,1024]{2,1,0:T(8,128)} async-done(((f32[2,1152,1024]{2,1,0:T(8,128)}), f32[2,1152,1024]{2,1,0:T(8,128)}) %all-reduce.2.cloned.1.call-update) | async-done | bytes 9437200 | tf_op jit(solution)/shard_map/psum | solution.py:45
  201.2 40.5 %all-gather.5.cloned.1.call-done = bf16[2,1152,1024]{2,1,0:T(8,128)(2,1)} async-done(((bf16[2,1152,128]{2,1,0:T(8,128)(2,1)}), bf16[2,1152,1024]{2,1,0:T(8,128)(2,1)}) %all-gather.5.cloned.1.call-update) | async-done | bytes 4718608 | tf_op jit(solution)/shard_map/all_gather | solution.py:47
  241.8 41.0 %all-gather.3.cloned.1.call-done = bf16[2,1152,1024]{2,1,0:T(8,128)(2,1)} async-done(((bf16[2,1152,128]{2,1,0:T(8,128)(2,1)}), bf16[2,1152,1024]{2,1,0:T(8,128)(2,1)}) %all-gather.3.cloned.1.call-update) | async-done | bytes 4718608 | tf_op jit(solution)/shard_map/all_gather | solution.py:48
  282.7 9.0 %multiply_convert_fusion = (bf16[2,1152,1024]{2,1,0:T(8,128)(2,1)S(1)}, bf16[2,1152,1024]{2,1,0:T(8,128)(2,1)S(1)}) fusion(f32[2,1152,1024]{2,1,0:T(8,128)} %all-reduce.2.cloned.1.call-done, bf16[2,1152,1024]{2,1,0:T(8,128)(2,1)} %all-gather.5.cloned.1.call-done, bf16[2,1152,1024]{2,1,0:T(8,128)(2,1)} %all-gather.3.cloned.1.call-done), kind=kLoop, calls=%fused_computation.13 | loop fusion | flops 35389440 | bytes 28311552 | tf_op jit(solution)/shard_map/convert_element_type | solution.py:56
  291.8 5.9 %fusion.30 = f32[2,1152,768]{2,1,0:T(8,128)} fusion(bf16[2,1152,1024]{2,1,0:T(8,128)(2,1)S(1)} %get-tuple-element.29, bf16[2,768,1024]{2,1,0:T(8,128)(2,1)S(1)} %copy-done.7), kind=kOutput, calls=%fused_computation.51 | convolution fusion | flops 3623878656 | bytes 14942208 | tf_op jit(solution)/shard_map/esh,edh->esd/dot_general | solution.py:67
  298.2 6.1 %add_convert_fusion = bf16[2,1152,768]{2,1,0:T(8,128)(2,1)S(1)} fusion(f32[2,1152,768]{2,1,0:T(8,128)} %fusion.30, bf16[2,1152,1024]{2,1,0:T(8,128)(2,1)S(1)} %get-tuple-element.28, bf16[2,768,1024]{2,1,0:T(8,128)(2,1)S(1)} %copy-done.8), kind=kOutput, calls=%fused_computation.16 | convolution fusion | flops 3627417600 | bytes 18481152 | tf_op jit(solution)/shard_map/esh,edh->esd/dot_general | solution.py:68
  304.3 13.9 %copy.112 = bf16[2,1152,768]{2,0,1:T(2,128)(2,1)} copy(bf16[2,1152,768]{2,1,0:T(8,128)(2,1)S(1)} %add_convert_fusion) | data formatting | bytes 7077888 | tf_op jit(solution)/shard_map/convert_element_type | solution.py:71
  318.2 9.3 %all-to-all-start.1 = ((bf16[2,128,9,768]{3,0,2,1:T(2,128)(2,1)}), bf16[2,128,9,768]{3,0,2,1:T(2,128)(2,1)}, u32[]{:S(2)}, u32[]{:S(2)}) async-start(bf16[2,128,9,768]{3,0,2,1:T(2,128)(2,1)} %bitcast.52), calls=%async_computation.1 | async-start | bytes 7077888 | tf_op jit(solution)/shard_map/all_to_all | solution.py:73
  327.5 9.4 %convert_bitcast_fusion = bf16[2,768,1024]{1,2,0:T(8,128)(2,1)} fusion(bf16[2,1152,1024]{2,1,0:T(8,128)(2,1)} %copy-done.2, bf16[2,1152,768]{2,1,0:T(8,128)(2,1)S(1)} %copy-done), kind=kOutput, calls=%fused_computation.19 | convolution fusion | flops 3625451520 | bytes 11403264 | tf_op jit(solution)/shard_map/esd,esh->edh/dot_general | solution.py:64
  337.0 4.6 %copy.119 = bf16[2,768,1024]{2,1,0:T(8,128)(2,1)} copy(bf16[2,768,1024]{1,2,0:T(8,128)(2,1)} %convert_bitcast_fusion) | data formatting | bytes 6291456
  341.6 9.4 %convert_bitcast_fusion.1 = bf16[2,768,1024]{1,2,0:T(8,128)(2,1)} fusion(bf16[2,1152,1024]{2,1,0:T(8,128)(2,1)} %copy-done.1, bf16[2,1152,768]{2,1,0:T(8,128)(2,1)S(1)} %copy-done), kind=kOutput, calls=%fused_computation.20 | convolution fusion | flops 3625451520 | bytes 11403264 | tf_op jit(solution)/shard_map/esd,esh->edh/dot_general | solution.py:61
  351.0 4.6 %copy.118 = bf16[2,768,1024]{2,1,0:T(8,128)(2,1)} copy(bf16[2,768,1024]{1,2,0:T(8,128)(2,1)} %convert_bitcast_fusion.1) | data formatting | bytes 6291456
  355.6 12.1 %fusion.13 = bf16[2,1024,768]{2,1,0:T(8,128)(2,1)} fusion(bf16[2,1152,768]{2,0,1:T(2,128)(2,1)} %bitcast.57, bf16[2,1152,1024]{2,1,0:T(8,128)(2,1)} %all-gather.3.cloned.1.call-done, bf16[2,1152,1024]{2,1,0:T(8,128)(2,1)} %all-gather.5.cloned.1.call-done), kind=kOutput, calls=%fused_computation.25 | convolution fusion | flops 3644325888 | bytes 16121856 | tf_op jit(solution)/shard_map/esh,esd->ehd/dot_general | solution.py:58
  367.8 5.5 %all-to-all-done.1 = bf16[2,128,9,768]{3,0,2,1:T(2,128)(2,1)} async-done(((bf16[2,128,9,768]{3,0,2,1:T(2,128)(2,1)}), bf16[2,128,9,768]{3,0,2,1:T(2,128)(2,1)}, u32[]{:S(2)}, u32[]{:S(2)}) %all-to-all-start.1) | async-done | bytes 3538976 | tf_op jit(solution)/shard_map/all_to_all | solution.py:73
  373.2 2.5 copy.113
  375.7 1.0 copy.125
  376.7 2.2 convolution_convert_fusion.1
  (29 shorter events, 3.7 us)
Async XLA Ops:
  7.2 320.4 %copy-start = (bf16[2,1152,768]{2,1,0:T(8,128)(2,1)S(1)}, bf16[2,1152,768]{2,1,0:T(8,128)(2,1)}, u32[]{:S(2)}) copy-start(bf16[2,1152,768]{2,1,0:T(8,128)(2,1)} %param.12) | copy-start | bytes 10616836
  7.2 194.1 %all-reduce.2.cloned.1.call-start = ((), (), s32[]{:S(2)}) async-start(), calls=%async_computation.2 | async-start | bytes 18874368 | tf_op jit(solution)/shard_map/psum | solution.py:45
  18.2 2.6 copy-start.4
  25.9 59.2 %copy-start.6 = (bf16[2,1024,768]{2,1,0:T(8,128)(2,1)S(1)}, bf16[2,1024,768]{2,1,0:T(8,128)(2,1)}, u32[]{:S(2)}) copy-start(bf16[2,1024,768]{2,1,0:T(8,128)(2,1)} %param.17) | copy-start | bytes 9437188
  83.2 1.9 copy-start.3
  91.3 150.4 %all-gather.5.cloned.1.call-start = ((), (), s32[]{:S(2)}) async-start(), calls=%async_computation.4 | async-start | bytes 5308416 | tf_op jit(solution)/shard_map/all_gather | solution.py:47
  92.1 190.6 %all-gather.3.cloned.1.call-start = ((), (), s32[]{:S(2)}) async-start(), calls=%async_computation.3 | async-start | bytes 5308416 | tf_op jit(solution)/shard_map/all_gather | solution.py:48
  282.7 9.1 %copy-start.7 = (bf16[2,768,1024]{2,1,0:T(8,128)(2,1)S(1)}, bf16[2,768,1024]{2,1,0:T(8,128)(2,1)}, u32[]{:S(2)}) copy-start(bf16[2,768,1024]{2,1,0:T(8,128)(2,1)} %param.15) | copy-start | bytes 9437188
  291.8 6.0 %copy-start.1 = (bf16[2,1152,1024]{2,1,0:T(8,128)(2,1)}, bf16[2,1152,1024]{2,1,0:T(8,128)(2,1)S(1)}, u32[]{:S(2)}) copy-start(bf16[2,1152,1024]{2,1,0:T(8,128)(2,1)S(1)} %get-tuple-element.29) | copy-start | bytes 14155780
  291.8 6.4 %copy-start.2 = (bf16[2,1152,1024]{2,1,0:T(8,128)(2,1)}, bf16[2,1152,1024]{2,1,0:T(8,128)(2,1)S(1)}, u32[]{:S(2)}) copy-start(bf16[2,1152,1024]{2,1,0:T(8,128)(2,1)S(1)} %get-tuple-element.28) | copy-start | bytes 14155780
  291.8 6.4 %copy-start.8 = (bf16[2,768,1024]{2,1,0:T(8,128)(2,1)S(1)}, bf16[2,768,1024]{2,1,0:T(8,128)(2,1)}, u32[]{:S(2)}) copy-start(bf16[2,768,1024]{2,1,0:T(8,128)(2,1)} %param.16) | copy-start | bytes 9437188
  318.2 55.0 %all-to-all-start.1 = ((bf16[2,128,9,768]{3,0,2,1:T(2,128)(2,1)}), bf16[2,128,9,768]{3,0,2,1:T(2,128)(2,1)}, u32[]{:S(2)}, u32[]{:S(2)}) async-start(bf16[2,128,9,768]{3,0,2,1:T(2,128)(2,1)} %bitcast.52), calls=%async_computation.1 | async-start | bytes 7077888 | tf_op jit(solution)/shard_map/all_to_all | solution.py:73
  375.7 1.0 copy-start.5
Sparse Core Ops, SparseCore 0:
  91.5 109.7 all-reduce.1
  202.9 38.8 all-gather.4
  243.5 39.2 all-gather.2
where the time goes:
time: 386 us; the launch traced here: 385 us
  waiting for transfers between devices  197 us (51%)
  blocking collectives  57.3 us (15%)
  matrix products  54 us (14%)
  local copies, waits for them, and re-layouts  40.1 us (10%)
  other arithmetic  13.9 us (4%)
  between operations  13.9 us (4%)
  starting transfers between devices  9.56 us (2%)
    psum x1, waiting for transfers between devices, body(): dhidden = lax.psum(partial_value, 'expert')  108 us
    all_to_all x1, blocking collectives, body(): lax.all_to_all(ordered, ('dp', 'expert'), split_axis=1, concat_axis=1, ti...  57.3 us
    all_gather x1, waiting for transfers between devices, body(): lax.all_gather(saved_up, 'expert', axis=2, tiled=True)  41 us
    all_gather x1, waiting for transfers between devices, body(): lax.all_gather(saved_gate, 'expert', axis=2, tiled=True)  40.5 us
    unnamed x23, local copies, waits for them, and re-layouts  15.2 us
    convert_element_type x1, local copies, waits for them, and re-layouts, body(): slot_grad = slot_grad.astype(jnp.bfloat16)  13.9 us
    dot_general x1, matrix products, body(): jnp.einsum('esh,esd->ehd', hidden, dispatched, preferred_element_type=jnp...  12.1 us
    dot_general x1, matrix products, body(): jnp.einsum('esd,esh->edh', saved_input, dup, preferred_element_type=jnp.f...  9.43 us
  transfers between devices with their start and end apart: 4, of which 4 were waited for; matrix products, arithmetic and copies ran while one was open for 10% of the time, Pallas kernels for 0%

commit v1 on v0

--- a/solution.py
+++ b/solution.py
@@ -42,7 +42,8 @@
     partial_value = jnp.einsum(
         "esd,ehd->esh", dispatched, w_down, preferred_element_type=jnp.float32
     )
-    dhidden = lax.psum(partial_value, "expert")
+    parts = lax.all_gather(partial_value, "expert")
+    dhidden = jnp.sum(parts, axis=0)
     gates_all, ups_all = (
         lax.all_gather(saved_gate, "expert", axis=2, tiled=True),
         lax.all_gather(saved_up, "expert", axis=2, tiled=True),

time: 386 us -> 606 us (1.57)
  waiting for transfers between devices: 197 us -> 387 us
  other arithmetic: 13.9 us -> 42.5 us
    all_gather x0 -> x1, waiting for transfers between devices: none -> 329 us  [body(): parts = lax.all_gather(partial_value, 'expert')]
    psum x1 -> x0, waiting for transfers between devices: 108 us -> none  [body(): dhidden = lax.psum(partial_value, 'expert')]
    all_gather x1, waiting for transfers between devices: 41 us -> 10.5 us  [body(): lax.all_gather(saved_up, 'expert', axis=2, tiled=True)]
    reduce_sum x0 -> x1, other arithmetic: none -> 28.6 us  [body(): dhidden = jnp.sum(parts, axis=0)]
  transfers between devices with their start and end apart: 4 -> 4, of which waited for: 4 -> 4; matrix products, arithmetic and copies ran while one was open for 10% -> 11% of each run, Pallas kernels for 0% -> 0%
where the time goes in v1:
time: 606 us; the launch traced here: 605 us
  waiting for transfers between devices  387 us (64%)
  blocking collectives  57.3 us (9%)
  matrix products  54.2 us (9%)
  other arithmetic  42.5 us (7%)
  local copies, waits for them, and re-layouts  40.2 us (7%)
  between operations  13.9 us (2%)
  starting transfers between devices  9.57 us (2%)
    all_gather x1, waiting for transfers between devices, body(): parts = lax.all_gather(partial_value, 'expert')  329 us
    all_to_all x1, blocking collectives, body(): lax.all_to_all(ordered, ('dp', 'expert'), split_axis=1, concat_axis=1, ti...  57.3 us
    all_gather x1, waiting for transfers between devices, body(): lax.all_gather(saved_gate, 'expert', axis=2, tiled=True)  41 us
    reduce_sum x1, other arithmetic, body(): dhidden = jnp.sum(parts, axis=0)  28.6 us
    unnamed x23, local copies, waits for them, and re-layouts  15.3 us
    convert_element_type x1, local copies, waits for them, and re-layouts, body(): slot_grad = slot_grad.astype(jnp.bfloat16)  13.9 us
    dot_general x1, matrix products, body(): jnp.einsum('esh,esd->ehd', hidden, dispatched, preferred_element_type=jnp...  12.2 us
  transfers between devices with their start and end apart: 4, of which 4 were waited for; matrix products, arithmetic and copies ran while one was open for 11% of the time, Pallas kernels for 0%

profile of v1, /device:TPU:1, one launch (start us, length us, event | category | flops | bytes accessed | tf_op | source)
XLA Modules:
  0.0 604.8 jit_solution(3678438772059396253)
XLA Ops:
  7.2 1.6 copy.105
  8.8 1.0 eq.45
  9.8 1.0 eq.41
  11.4 1.9 reduce-window.6
  13.3 0.9 slice_reduce_fusion
  14.2 0.9 fusion.24
  15.1 0.8 reduce_sum.30
  15.9 0.9 copy.108
  18.2 2.6 convolution_convert_fusion
  20.8 1.0 copy.124
  22.2 3.6 copy.110
  25.9 57.3 %all_to_all.10 = bf16[2,128,9,768]{3,0,2,1:T(2,128)(2,1)S(1)} all-to-all(bf16[2,128,9,768]{3,0,2,1:T(2,128)(2,1)S(1)} %copy.110), channel_id=1, replica_groups=mesh['dp'=16,'expert'=8] {'dp','expert'}, dimensions={1} | all-to-all | bytes 7077888 | tf_op jit(solution)/shard_map/all_to_all | solution.py:40
  83.2 2.0 copy-done.3
  85.2 6.2 %fusion.11 = f32[2,1152,1024]{2,1,0:T(8,128)} fusion(bf16[2,1024,768]{2,1,0:T(8,128)(2,1)S(1)} %copy-done.6, bf16[2,1152,768]{2,0,1:T(2,128)(2,1)S(1)} %bitcast.57), kind=kOutput, calls=%fused_computation.23 | convolution fusion | flops 3623878656 | bytes 16121856 | tf_op jit(solution)/shard_map/esd,ehd->esh/dot_general | solution.py:42
  93.0 329.1 %all-gather.9.cloned.1.call-done = f32[16,1152,1024]{2,1,0:T(8,128)} async-done(((f32[2,1152,1024]{2,1,0:T(8,128)}), f32[16,1152,1024]{2,1,0:T(8,128)}) %all-gather.9.cloned.1.call-update) | async-done | bytes 75497488 | tf_op jit(solution)/shard_map/all_gather | solution.py:45
  422.1 28.6 %reduce_sum.32 = f32[2,1152,1024]{2,1,0:T(8,128)} reduce(f32[8,2,1152,1024]{3,2,1,0:T(8,128)} %bitcast.4, f32[]{:T(128)} %constant.38.clone.1), dimensions={0}, to_apply=%region_4.5 | reduce | flops 16515072 | bytes 84934656 | tf_op jit(solution)/shard_map/reduce_sum | solution.py:46
  450.7 10.5 %all-gather.5.cloned.1.call-done = bf16[2,1152,1024]{2,1,0:T(8,128)(2,1)} async-done(((bf16[2,1152,128]{2,1,0:T(8,128)(2,1)}), bf16[2,1152,1024]{2,1,0:T(8,128)(2,1)}) %all-gather.5.cloned.1.call-update) | async-done | bytes 4718608 | tf_op jit(solution)/shard_map/all_gather | solution.py:49
  461.2 41.0 %all-gather.7.cloned.1.call-done = bf16[2,1152,1024]{2,1,0:T(8,128)(2,1)} async-done(((bf16[2,1152,128]{2,1,0:T(8,128)(2,1)}), bf16[2,1152,1024]{2,1,0:T(8,128)(2,1)}) %all-gather.7.cloned.1.call-update) | async-done | bytes 4718608 | tf_op jit(solution)/shard_map/all_gather | solution.py:48
  502.1 9.0 %multiply_convert_fusion = (bf16[2,1152,1024]{2,1,0:T(8,128)(2,1)S(1)}, bf16[2,1152,1024]{2,1,0:T(8,128)(2,1)S(1)}) fusion(f32[2,1152,1024]{2,1,0:T(8,128)} %reduce_sum.32, bf16[2,1152,1024]{2,1,0:T(8,128)(2,1)} %all-gather.7.cloned.1.call-done, bf16[2,1152,1024]{2,1,0:T(8,128)(2,1)} %all-gather.5.cloned.1.call-done), kind=kLoop, calls=%fused_computation.13 | loop fusion | flops 35389440 | bytes 28311552 | tf_op jit(solution)/shard_map/convert_element_type | solution.py:57
  511.2 5.9 fusion.30
  517.6 6.1 %add_convert_fusion = bf16[2,1152,768]{2,1,0:T(8,128)(2,1)S(1)} fusion(f32[2,1152,768]{2,1,0:T(8,128)} %fusion.30, bf16[2,1152,1024]{2,1,0:T(8,128)(2,1)S(1)} %get-tuple-element.28, bf16[2,768,1024]{2,1,0:T(8,128)(2,1)S(1)} %copy-done.8), kind=kOutput, calls=%fused_computation.16 | convolution fusion | flops 3627417600 | bytes 18481152 | tf_op jit(solution)/shard_map/esh,edh->esd/dot_general | solution.py:69
  523.7 13.9 %copy.112 = bf16[2,1152,768]{2,0,1:T(2,128)(2,1)} copy(bf16[2,1152,768]{2,1,0:T(8,128)(2,1)S(1)} %add_convert_fusion) | data formatting | bytes 7077888 | tf_op jit(solution)/shard_map/convert_element_type | solution.py:72
  537.6 9.3 %all-to-all-start.1 = ((bf16[2,128,9,768]{3,0,2,1:T(2,128)(2,1)}), bf16[2,128,9,768]{3,0,2,1:T(2,128)(2,1)}, u32[]{:S(2)}, u32[]{:S(2)}) async-start(bf16[2,128,9,768]{3,0,2,1:T(2,128)(2,1)} %bitcast.53), calls=%async_computation.1 | async-start | bytes 7077888 | tf_op jit(solution)/shard_map/all_to_all | solution.py:74
  546.9 12.2 %fusion.13 = bf16[2,1024,768]{2,1,0:T(8,128)(2,1)} fusion(bf16[2,1152,768]{2,0,1:T(2,128)(2,1)} %bitcast.58, bf16[2,1152,1024]{2,1,0:T(8,128)(2,1)} %all-gather.5.cloned.1.call-done, bf16[2,1152,1024]{2,1,0:T(8,128)(2,1)} %all-gather.7.cloned.1.call-done), kind=kOutput, calls=%fused_computation.25 | convolution fusion | flops 3644325888 | bytes 16121856 | tf_op jit(solution)/shard_map/esh,esd->ehd/dot_general | solution.py:59
  559.1 9.4 %convert_bitcast_fusion.1 = bf16[2,768,1024]{1,2,0:T(8,128)(2,1)} fusion(bf16[2,1152,1024]{2,1,0:T(8,128)(2,1)} %copy-done.2, bf16[2,1152,768]{2,1,0:T(8,128)(2,1)S(1)} %copy-done), kind=kOutput, calls=%fused_computation.20 | convolution fusion | flops 3625451520 | bytes 11403264 | tf_op jit(solution)/shard_map/esd,esh->edh/dot_general | solution.py:62
  568.5 4.6 copy.118
  573.1 9.6 %convert_bitcast_fusion = bf16[2,768,1024]{1,2,0:T(8,128)(2,1)} fusion(bf16[2,1152,1024]{2,1,0:T(8,128)(2,1)} %copy-done.1, bf16[2,1152,768]{2,1,0:T(8,128)(2,1)S(1)} %copy-done), kind=kOutput, calls=%fused_computation.19 | convolution fusion | flops 3625451520 | bytes 11403264 | tf_op jit(solution)/shard_map/esd,esh->edh/dot_general | solution.py:65
  582.7 4.6 copy.119
  587.3 5.3 all-to-all-done.1
  592.6 2.5 copy.113
  595.1 1.0 copy.125
  596.1 2.2 convolution_convert_fusion.1
  (30 shorter events, 4.5 us)
Async XLA Ops:
  7.2 551.9 %copy-start = (bf16[2,1152,768]{2,1,0:T(8,128)(2,1)S(1)}, bf16[2,1152,768]{2,1,0:T(8,128)(2,1)}, u32[]{:S(2)}) copy-start(bf16[2,1152,768]{2,1,0:T(8,128)(2,1)} %param.12) | copy-start | bytes 10616836
  7.2 414.9 %all-gather.9.cloned.1.call-start = ((), (), s32[]{:S(2)}) async-start(), calls=%async_computation.4 | async-start | bytes 84934656 | tf_op jit(solution)/shard_map/all_gather | solution.py:45
  17.5 3.3 copy-start.4
  25.9 59.3 %copy-start.6 = (bf16[2,1024,768]{2,1,0:T(8,128)(2,1)S(1)}, bf16[2,1024,768]{2,1,0:T(8,128)(2,1)}, u32[]{:S(2)}) copy-start(bf16[2,1024,768]{2,1,0:T(8,128)(2,1)} %param.17) | copy-start | bytes 9437188
  83.2 2.0 copy-start.3
  91.5 369.7 %all-gather.5.cloned.1.call-start = ((), (), s32[]{:S(2)}) async-start(), calls=%async_computation.2 | async-start | bytes 5308416 | tf_op jit(solution)/shard_map/all_gather | solution.py:49
  92.2 409.9 %all-gather.7.cloned.1.call-start = ((), (), s32[]{:S(2)}) async-start(), calls=%async_computation.3 | async-start | bytes 5308416 | tf_op jit(solution)/shard_map/all_gather | solution.py:48
  502.1 9.1 %copy-start.7 = (bf16[2,768,1024]{2,1,0:T(8,128)(2,1)S(1)}, bf16[2,768,1024]{2,1,0:T(8,128)(2,1)}, u32[]{:S(2)}) copy-start(bf16[2,768,1024]{2,1,0:T(8,128)(2,1)} %param.15) | copy-start | bytes 9437188
  511.2 6.0 copy-start.2
  511.2 6.4 %copy-start.1 = (bf16[2,1152,1024]{2,1,0:T(8,128)(2,1)}, bf16[2,1152,1024]{2,1,0:T(8,128)(2,1)S(1)}, u32[]{:S(2)}) copy-start(bf16[2,1152,1024]{2,1,0:T(8,128)(2,1)S(1)} %get-tuple-element.28) | copy-start | bytes 14155780
  511.2 6.4 %copy-start.8 = (bf16[2,768,1024]{2,1,0:T(8,128)(2,1)S(1)}, bf16[2,768,1024]{2,1,0:T(8,128)(2,1)}, u32[]{:S(2)}) copy-start(bf16[2,768,1024]{2,1,0:T(8,128)(2,1)} %param.16) | copy-start | bytes 9437188
  537.6 55.0 %all-to-all-start.1 = ((bf16[2,128,9,768]{3,0,2,1:T(2,128)(2,1)}), bf16[2,128,9,768]{3,0,2,1:T(2,128)(2,1)}, u32[]{:S(2)}, u32[]{:S(2)}) async-start(bf16[2,128,9,768]{3,0,2,1:T(2,128)(2,1)} %bitcast.53), calls=%async_computation.1 | async-start | bytes 7077888 | tf_op jit(solution)/shard_map/all_to_all | solution.py:74
  595.1 1.0 copy-start.5
Sparse Core Ops, SparseCore 0:
  91.6 330.4 all-gather.8
  423.8 37.3 all-gather.4
  462.9 39.2 all-gather.6
